TPU v7x, 256 devices: a whole 4x4x8 slice. The times are simulated.
256 devices in a mesh: lon: 32 (over z, y), lat: 8 (over x, core).
Axes of the slice: x: 4, y: 4, z: 8, core: 2. Of those that a mesh axis runs over, the one named last changes fastest.
Arguments:
- right_side: float32 [2048, 16384], P('lat', 'lon'), may hold values from -6 to 6
- depth_level: int32 [2048, 16384], P('lat', 'lon'), may hold values from 1 to 50
- ocean_mask: int32 [2048, 16384], P('lat', 'lon'), may hold values 0 or 1
Outputs:
- pressure: float32 [2048, 16384], P('lat', 'lon')
- residual: float32 [2048, 16384], P('lat', 'lon')
All inputs are finite; a program needn't handle non-finite values. No bound on the sum of `ocean_mask` on one device may be relied on, other than what follows from the above.
Results may differ from a plain program's by a relative error of at most 0.0003.
Values sent between devices are 32-bit elements; how exact they have to be, the bound alone decides.
No kernel may reach another device: no remote copies, remote signals or barrier semaphores. Data moves between devices by JAX's collectives and lax.ppermute only.
A program may use at most 128 MiB of HBM per device.

v0:
```python
import jax
import jax.numpy as jnp
import numpy as np
from jax import lax
from jax.experimental import pallas as pl
from jax.experimental.pallas import tpu as pltpu
from jax.sharding import PartitionSpec as P

LEVELS = 4
COARSE_SWEEPS = 9
DEPTH_LEVELS = 50
OMEGA = 0.8
SIGMA = 1e-05

CELL = 2 ** (LEVELS - 1)
LANES = 128
SIDE = 128
PAD = SIDE // CELL
EDGE = 4
FAR = 8
ROWS = 32
COLS = 64
TALL = ROWS + 2 * EDGE
STRIP = EDGE * CELL


def east(x):
    return pltpu.roll(x, x.shape[1] - 1, 1)


def west(x):
    return pltpu.roll(x, 1, 1)


def north(x):
    return pltpu.roll(x, x.shape[0] - 1, 0)


def south(x):
    return pltpu.roll(x, 1, 0)


def each(count, body):
    if count <= 2:
        for q in range(count):
            body(q)
    else:
        lax.fori_loop(0, count, lambda q, carry: (body(q), carry)[1], 0)


def whole(ref, q, r):
    return ref[q, r]


def ends(ref, q, r):
    return jnp.concatenate([ref[q, r, 0:8, :], ref[q, r, TALL - 8 : TALL, :]], axis=0)


def close(v, n):
    for r in range(n):
        v[0, r] = south(v[n, r])
        v[n + 1, r] = north(v[1, r])


def find_faces(n, h, ke, kn):
    for r in range(n):
        h[n, r] = north(h[0, r])

    def body(q):
        for r in range(n):
            here = h[q, r]
            ke[q, r] = jnp.minimum(here, h[q, r + 1] if r + 1 < n else east(h[q, 0]))
            kn[q + 1, r] = jnp.minimum(here, h[q + 1, r])

    each(n, body)
    for r in range(n):
        kn[0, r] = south(kn[n, r])


def weigh(faces, source):
    diagonal = SIGMA + faces
    return diagonal, OMEGA / diagonal, jnp.where(faces > 0.0, source, 0.0)


def find_weights(n, ke, kn, source, d, w, s, v=None):
    def body(q):
        for r in range(n):
            kw = ke[q, r - 1] if r else west(ke[q, n - 1])
            faces = (ke[q, r] + kw) + (kn[q + 1, r] + kn[q, r])
            diagonal, weight, kept = weigh(faces, source[q, r])
            d[q, r], w[q, r], s[q, r] = diagonal, weight, kept
            if v is not None:
                v[q + 1, r] = weight * kept

    each(n, body)
    if v is not None:
        close(v, n)


def start(n, w, s, v, get):
    def body(q):
        for r in range(n):
            v[q + 1, r] = get(w, q, r) * get(s, q, r)

    each(n, body)
    close(v, n)


def pull(n, ke, kn, v, q, get):
    ks = [get(ke, q, r) for r in range(n)]
    cs = [v[q + 1, r] for r in range(n)]
    out = []
    for r in range(n):
        kw = ks[r - 1] if r else west(ks[n - 1])
        ve = cs[r + 1] if r + 1 < n else east(cs[0])
        vw = cs[r - 1] if r else west(cs[n - 1])
        out.append(
            (ks[r] * ve + kw * vw)
            + (get(kn, q + 1, r) * v[q + 2, r] + get(kn, q, r) * v[q, r])
        )
    return cs, out


def sweep(n, ke, kn, w, s, v, out, get=whole, also=None):
    def body(q):
        cs, total = pull(n, ke, kn, v, q, get)
        for r in range(n):
            new = (1.0 - OMEGA) * cs[r] + get(w, q, r) * (get(s, q, r) + total[r])
            out[q + 1, r] = new
            if also is not None:
                also(q, r, new)

    each(n, body)
    close(out, n)


def remains(n, ke, kn, d, s, v, q, get):
    cs, total = pull(n, ke, kn, v, q, get)
    return [(get(s, q, r) - get(d, q, r) * cs[r]) + total[r] for r in range(n)]


def restrict(n, ke, kn, d, s, v, get, put):
    def body(q):
        a = remains(n, ke, kn, d, s, v, 2 * q, get)
        b = remains(n, ke, kn, d, s, v, 2 * q + 1, get)
        for r in range(n // 2):
            put(q, r, 0.25 * ((a[2 * r] + a[2 * r + 1]) + (b[2 * r] + b[2 * r + 1])))

    each(n // 2, body)


def coarsen(n, h, put):
    def body(q):
        for r in range(n // 2):
            a = h[2 * q, 2 * r] + h[2 * q, 2 * r + 1]
            b = h[2 * q + 1, 2 * r] + h[2 * q + 1, 2 * r + 1]
            put(q, r, 0.0625 * (a + b))

    each(n // 2, body)


def merged(inner, strips):
    row = lax.broadcasted_iota(jnp.int32, (8, LANES), 0)
    low = jnp.where(row < 6, strips[0:8], inner[0:8])
    high = jnp.where(row >= 2, strips[8:16], inner[TALL - 8 : TALL])
    return jnp.concatenate([low, inner[8 : TALL - 8], high], axis=0)


def dot_parts(x, matrix):
    high = x.astype(jnp.bfloat16)
    low = (x - high.astype(jnp.float32)).astype(jnp.bfloat16)
    return jnp.dot(high, matrix, preferred_element_type=jnp.float32) + jnp.dot(
        low, matrix, preferred_element_type=jnp.float32
    )


def pack_kernel(f_l, f_r, d_l, d_r, m_l, m_r, first, second):
    def fill(to_next, to_previous):
        to_next[0] = f_r[...]
        to_next[1] = (d_r[...] * m_r[...]).astype(jnp.float32)
        to_previous[0] = f_l[...]
        to_previous[1] = (d_l[...] * m_l[...]).astype(jnp.float32)

    even = lax.rem(lax.axis_index("lon"), 2) == 0

    @pl.when(even)
    def _():
        fill(first, second)

    @pl.when(jnp.logical_not(even))
    def _():
        fill(second, first)


def down_kernel(
    f, depth, mask, first, second, split,
    s0, h0, it0, s1, it1, s2, it2, s3, out_first, out_second,
    nat_s, nat_h, h1, h2, ke0, kn0, d0, w0, k0, v0,
    ke1, kn1, d1, w1, k1, v1, ke2, kn2, d2, w2, k2, v2,
):
    even = lax.rem(lax.axis_index("lon"), 2) == 0
    matrix = split[...]
    nothing = jnp.zeros((CELL, STRIP, LANES), jnp.float32)
    for nat in (nat_s, nat_h):
        nat[:, 0:STRIP, :] = nothing
        nat[:, STRIP + ROWS * CELL : TALL * CELL, :] = nothing

    def keep(nat, x):
        for r in range(CELL):
            nat[r, STRIP : STRIP + ROWS * CELL, :] = x[:, r * LANES : (r + 1) * LANES]

    def sides(i):
        a, b = first[i], second[i]
        return jnp.where(even, b, a), jnp.where(even, a, b)

    before, after = sides(0)
    keep(nat_s, dot_parts(jnp.concatenate([before, f[...], after], axis=1), matrix))
    before, after = sides(1)
    level = (depth[...] * mask[...]).astype(jnp.float32)
    level = jnp.concatenate([before, level, after], axis=1).astype(jnp.bfloat16)
    level = jnp.dot(level, matrix, preferred_element_type=jnp.float32)
    keep(nat_h, level * (1.0 / DEPTH_LEVELS))

    for q in range(CELL):
        rows = pl.ds(q, TALL, stride=CELL)
        for r in range(CELL):
            s0[q, r] = nat_s[r, rows, :]
            h0[q, r] = nat_h[r, rows, :]

    def put(ref):
        def at(q, r, x):
            ref[q, r] = x

        return at

    s_next, h_next, h3 = (s1, s2, None), (h1, h2, None), []
    source3 = []
    for i, (n, h, ke, kn, source, d, w, k, v, it) in enumerate(
        (
            (8, h0, ke0, kn0, s0, d0, w0, k0, v0, it0),
            (4, h1, ke1, kn1, s1, d1, w1, k1, v1, it1),
            (2, h2, ke2, kn2, s2, d2, w2, k2, v2, it2),
        )
    ):
        find_faces(n, h, ke, kn)
        find_weights(n, ke, kn, source, d, w, k, v)
        sweep(n, ke, kn, w, k, v, it)
        if i < 2:
            restrict(n, ke, kn, d, k, it, whole, put(s_next[i]))
            coarsen(n, h, put(h_next[i]))
        else:
            restrict(n, ke, kn, d, k, it, whole, lambda q, r, x: source3.append(x))
            coarsen(n, h, lambda q, r, x: h3.append(x))
    s3[...] = source3[0]

    def send(to, row, blocks):
        to[:, 0:STRIP, :] = nat_s[:, row : row + STRIP, :]
        to[:, STRIP : 2 * STRIP, :] = nat_h[:, row : row + STRIP, :]
        for i in range(CELL):
            to[i, 2 * STRIP : 2 * STRIP + 8, :] = blocks[i] if i < len(blocks) else jnp.zeros((8, LANES), jnp.float32)

    s, h = source3[0], h3[0]

    def fill(to_next, to_previous):
        send(to_next, ROWS * CELL, (s[24:32], s[32:40], h[24:32]))
        send(to_previous, STRIP, (s[8:16], s[0:8], h[8:16]))

    even = lax.rem(lax.axis_index("lat"), 2) == 0

    @pl.when(even)
    def _():
        fill(out_first, out_second)

    @pl.when(jnp.logical_not(even))
    def _():
        fill(out_second, out_first)


def up_kernel(
    s0_in, h0_in, it0_in, s1_in, it1_in, s2_in, it2_in, s3_in, first, second, join,
    pressure, residual,
    far, s0, h0, s1, h1, s2, h2, ke0, kn0, d0, w0, k0, e0, g0, a0, b0,
    ke1, kn1, d1, w1, k1, e1, g1, a1, b1, ke2, kn2, d2, w2, k2, e2, g2, a2, b2, flat, nat,
):
    even = lax.rem(lax.axis_index("lat"), 2) == 0
    tops = slice(TALL - EDGE, TALL)

    def own(q):
        for r in range(CELL):
            s0[q, r] = s0_in[q, r]
            h0[q, r] = h0_in[q, r]

    each(CELL, own)

    def fill(low, high):
        for q in range(CELL):
            for r in range(CELL):
                s0[q, r, 0:EDGE, :] = low[r, pl.ds(q, EDGE, stride=CELL), :]
                s0[q, r, tops, :] = high[r, pl.ds(q, EDGE, stride=CELL), :]
                h0[q, r, 0:EDGE, :] = low[r, pl.ds(STRIP + q, EDGE, stride=CELL), :]
                h0[q, r, tops, :] = high[r, pl.ds(STRIP + q, EDGE, stride=CELL), :]
        for i in range(3):
            far[0, i] = low[i, 2 * STRIP : 2 * STRIP + 8, :]
            far[1, i] = high[i, 2 * STRIP : 2 * STRIP + 8, :]

    @pl.when(even)
    def _():
        fill(second, first)

    @pl.when(jnp.logical_not(even))
    def _():
        fill(first, second)

    levels = (
        (8, h0, ke0, kn0, s0, d0, w0, k0, e0, g0, a0, b0, it0_in),
        (4, h1, ke1, kn1, s1, d1, w1, k1, e1, g1, a1, b1, it1_in),
        (2, h2, ke2, kn2, s2, d2, w2, k2, e2, g2, a2, b2, it2_in),
    )
    h3, source3 = [], []
    for i, (n, h, ke, kn, source, d, w, k, e, g, _, _, _) in enumerate(levels):
        find_faces(n, h, ke, kn)
        find_weights(n, ke, kn, source, d, w, k)
        start(n, w, k, e, ends)
        sweep(n, ke, kn, w, k, e, g, ends)
        if i < 2:
            s_next, s_inner, h_next = ((s1, s1_in, h1), (s2, s2_in, h2))[i]

            def put_s(q, r, x, s_next=s_next, s_inner=s_inner):
                s_next[q, r] = merged(s_inner[q, r], x)

            def put_h(q, r, x, h_next=h_next):
                h_next[q, r] = x

            restrict(n, ke, kn, d, k, g, ends, put_s)
            coarsen(n, h, put_h)
        else:
            restrict(n, ke, kn, d, k, g, ends, lambda q, r, x: source3.append(merged(s3_in[...], x)))
            coarsen(n, h, lambda q, r, x: h3.append(x))

    row = lax.broadcasted_iota(jnp.int32, (8, LANES), 0)
    s, h = source3[0], h3[0]
    s = jnp.concatenate(
        [
            far[0, 0],
            jnp.where(row < 2, far[0, 1], s[0:8]),
            s[8 : TALL - 8],
            jnp.where(row >= 6, far[1, 1], s[TALL - 8 : TALL]),
            far[1, 0],
        ],
        axis=0,
    )
    h = jnp.concatenate([far[0, 2], h, far[1, 2]], axis=0)
    ke, kn = jnp.minimum(h, east(h)), jnp.minimum(h, north(h))
    kw, ks = west(ke), south(kn)
    _, weight, s = weigh((ke + kw) + (kn + ks), s)
    v = weight * s
    for _ in range(COARSE_SWEEPS - 1):
        total = (ke * east(v) + kw * west(v)) + (kn * north(v) + ks * south(v))
        v = (1.0 - OMEGA) * v + weight * (s + total)
    coarse = v[FAR : FAR + TALL]

    above = lambda q, r: coarse
    for n, h, ke, kn, source, d, w, k, e, g, a, b, inner in reversed(levels):

        def correct(q, n=n, g=g, a=a, inner=inner, above=above):
            for r in range(n):
                a[q + 1, r] = merged(inner[q + 1, r], g[q + 1, r]) + above(q, r)

        each(n, correct)
        close(a, n)
        sweep(n, ke, kn, w, k, a, b)
        if n < CELL:
            sweep(n, ke, kn, w, k, b, a)
        above = lambda q, r, a=a: a[lax.div(q, 2) + 1, r // 2]

    n, _, ke, kn, _, d, w, k, _, _, a, b, _ = levels[0]

    def flatten(q, r, x):
        flat[pl.ds(pl.multiple_of(q * TALL, 8), TALL), r * LANES : (r + 1) * LANES] = x

    def finish(out):
        res = dot_parts(flat[...], join[...])
        for c in range(nat.shape[0]):
            lanes = slice(c * LANES, (c + 1) * LANES)
            for q in range(CELL):
                nat[c, pl.ds(q, TALL, stride=CELL), :] = res[q * TALL : (q + 1) * TALL, lanes]
            out[:, lanes] = nat[c, STRIP : STRIP + ROWS * CELL, :]

    sweep(n, ke, kn, w, k, b, a, whole, flatten)
    finish(pressure)

    def last(q):
        for r, x in enumerate(remains(n, ke, kn, d, k, a, q, whole)):
            flatten(q, r, x)

    each(n, last)
    finish(residual)


def swap(x, axis, count, offset, closed):
    pairs = []
    for i in range(offset, count, 2):
        if i + 1 < count or closed:
            j = (i + 1) % count
            pairs += [(i, j), (j, i)]
    return lax.ppermute(x, axis, pairs)


def split_matrix(columns):
    out = np.zeros((columns + 2 * SIDE, CELL * LANES), np.float32)
    c = np.arange(columns + 2 * SIDE)
    out[c, (c % CELL) * LANES + c // CELL] = 1.0
    return jnp.asarray(out, jnp.bfloat16)


def join_matrix(columns):
    out = np.zeros((CELL * LANES, columns), np.float32)
    c = np.arange(columns)
    out[(c % CELL) * LANES + c // CELL + PAD, c] = 1.0
    return jnp.asarray(out, jnp.bfloat16)


VMEM = pl.BlockSpec(memory_space=pltpu.VMEM)


def shaped(*dims):
    return jax.ShapeDtypeStruct(dims, jnp.float32)


def planes(n, more=0, rows=TALL):
    return (n + more, n, rows, LANES)


def buffers(*shapes):
    return [pltpu.VMEM(s, jnp.float32) for s in shapes]


LIMIT = pltpu.CompilerParams(vmem_limit_bytes=48 * 1024 * 1024)


def local(right_side, depth_level, ocean_mask):
    rows, columns = right_side.shape
    lon, lat = lax.axis_size("lon"), lax.axis_size("lat")
    left = pl.BlockSpec((rows, SIDE), lambda i: (0, 0))
    right = pl.BlockSpec((rows, SIDE), lambda i: (0, columns // SIDE - 1))
    first, second = pl.pallas_call(
        pack_kernel,
        grid=(1,),
        out_shape=[shaped(2, rows, SIDE)] * 2,
        in_specs=[left, right] * 3,
        out_specs=[VMEM] * 2,
    )(right_side, right_side, depth_level, depth_level, ocean_mask, ocean_mask)
    first = swap(first, "lon", lon, 0, True)
    second = swap(second, "lon", lon, 1, True)

    wide = CELL * LANES
    message = shaped(CELL, 2 * STRIP + 8, LANES)
    outs = pl.pallas_call(
        down_kernel,
        out_shape=[
            shaped(*planes(8)), shaped(*planes(8, 1)), shaped(*planes(8, 2)),
            shaped(*planes(4)), shaped(*planes(4, 2)),
            shaped(*planes(2)), shaped(*planes(2, 2)),
            shaped(TALL, LANES), message, message,
        ],
        in_specs=[VMEM] * 6,
        out_specs=[VMEM] * 10,
        scratch_shapes=buffers(
            (CELL, TALL * CELL, LANES), (CELL, TALL * CELL, LANES), planes(4, 1), planes(2, 1),
            *[s for n in (8, 4, 2) for s in (planes(n), planes(n, 1), planes(n), planes(n), planes(n), planes(n, 2))],
        ),
        compiler_params=LIMIT,
    )(right_side, depth_level, ocean_mask, first, second, split_matrix(columns))
    *fields, first, second = outs
    first = swap(first, "lat", lat, 0, False)
    second = swap(second, "lat", lat, 1, False)
    return pl.pallas_call(
        up_kernel,
        out_shape=[shaped(rows, columns)] * 2,
        in_specs=[VMEM] * 11,
        out_specs=[VMEM] * 2,
        scratch_shapes=buffers(
            (2, 3, 8, LANES),
            *[s for n in (8, 4, 2) for s in (planes(n), planes(n, 1))],
            *[
                s
                for n in (8, 4, 2)
                for s in (
                    planes(n), planes(n, 1), planes(n), planes(n), planes(n),
                    planes(n, 2, 16), planes(n, 2, 16), planes(n, 2), planes(n, 2),
                )
            ],
            (TALL * CELL, wide), (columns // LANES, TALL * CELL, LANES),
        ),
        compiler_params=LIMIT,
    )(*fields, first, second, join_matrix(columns))


def solution(mesh):
    placed = (P("lat", "lon"), P("lat", "lon"), P("lat", "lon"))
    return jax.shard_map(
        local,
        mesh=mesh,
        in_specs=placed,
        out_specs=(P("lat", "lon"), P("lat", "lon")),
        check_vma=False,
    )
```

profile of v0, /device:TPU:1, one launch (start us, length us, event | category | flops | bytes accessed | tf_op | source)
XLA Modules:
  0.0 50.7 jit_solution(11385398761538289149)
XLA Ops:
  0.6 0.0 copy-start.2
  0.6 0.0 copy-start.1
  0.6 0.0 copy-start
  0.7 2.2 %shard_map.68 = (f32[2,256,128]{2,1,0:T(8,128)}, f32[2,256,128]{2,1,0:T(8,128)}) custom-call(f32[256,512]{1,0:T(8,128)} %f.1, f32[256,512]{1,0:T(8,128)} %f.1, s32[256,512]{1,0:T(8,128)} %depth.1, s32[256,512]{1,0:T(8,128)} %depth.1, s32[256,512]{1,0:T(8,128)} %mask.1, s32[256,512]{1,0:T(8,128)} %mask.1), custom_call_target="tpu_custom_call" | custom-call | tf_op jit(solution)/shard_map/pallas_call | solution.py:446
  2.8 2.1 %collective-permute-start = (f32[2,256,128]{2,1,0:T(8,128)}, f32[2,256,128]{2,1,0:T(8,128)S(1)}, u32[]{:S(2)}, u32[]{:S(2)}) collective-permute-start(f32[2,256,128]{2,1,0:T(8,128)} %get-tuple-element.14), channel_id=1, source_target_pairs={{0,8},{8,0},{16,24},{24,16},{32,40},{40,32},{48,56},{56,48},{64,72... | collective-permute-start | bytes 786440 | tf_op jit(solution)/shard_map/ppermute | solution.py:406
  4.9 0.0 copy-start.4
  4.9 7.2 %collective-permute-start.1 = (f32[2,256,128]{2,1,0:T(8,128)}, f32[2,256,128]{2,1,0:T(8,128)S(1)}, u32[]{:S(2)}, u32[]{:S(2)}) collective-permute-start(f32[2,256,128]{2,1,0:T(8,128)} %get-tuple-element.15), channel_id=1, source_target_pairs={{8,16},{16,8},{24,32},{32,24},{40,48},{48,40},{56,64},{64,56},{72,... | collective-permute-start | bytes 786440 | tf_op jit(solution)/shard_map/ppermute | solution.py:406
  12.1 0.0 collective-permute-done.first
  12.1 5.9 %collective-permute-done.1.second = f32[2,256,128]{2,1,0:T(8,128)S(1)} collective-permute-done((f32[2,256,128]{2,1,0:T(8,128)}, f32[2,256,128]{2,1,0:T(8,128)S(1)}, u32[]{:S(2)}, u32[]{:S(2)}) %collective-permute-start.1) | collective-permute-done | bytes 262176 | tf_op jit(solution)/shard_map/ppermute | solution.py:406
  18.1 0.0 copy-done.2
  18.1 0.0 copy-done.1
  18.1 0.0 copy-done
  18.1 9.0 %shard_map.69 = (f32[8,8,40,128]{3,2,1,0:T(8,128)S(1)}, f32[9,8,40,128]{3,2,1,0:T(8,128)}, f32[10,8,40,128]{3,2,1,0:T(8,128)}, f32[4,4,40,128]{3,2,1,0:T(8,128)S...) custom-call(f32[256,512]{1,0:T(8,128)S(1)} %copy-done, ...), custom_call_target="tpu_custom_call" | custom-call | tf_op jit(solution)/shard_map/pallas_call | solution.py:458
  27.1 1.5 %collective-permute-start.2 = (f32[8,72,128]{2,1,0:T(8,128)S(1)}, f32[8,72,128]{2,1,0:T(8,128)S(1)}, u32[]{:S(2)}, u32[]{:S(2)}) collective-permute-start(f32[8,72,128]{2,1,0:T(8,128)S(1)} %get-tuple-element.24), channel_id=1, source_target_pairs={{0,1},{1,0},{2,3},{3,2},{4,5},{5,4},{6,7},{7,6},{8,9},{9,8},{10,11... | collective-permute-start | bytes 884744 | tf_op jit(solution)/shard_map/ppermute | solution.py:406
  28.6 3.0 %collective-permute-start.3 = (f32[8,72,128]{2,1,0:T(8,128)S(1)}, f32[8,72,128]{2,1,0:T(8,128)S(1)}, u32[]{:S(2)}, u32[]{:S(2)}) collective-permute-start(f32[8,72,128]{2,1,0:T(8,128)S(1)} %get-tuple-element.25), channel_id=1, source_target_pairs={{1,2},{2,1},{3,4},{4,3},{5,6},{6,5},{9,10},{10,9},{11,12},{12,11},... | collective-permute-start | bytes 884744 | tf_op jit(solution)/shard_map/ppermute | solution.py:406
  31.6 0.0 collective-permute-done.2.first
  31.6 5.0 %collective-permute-done.3.second = f32[8,72,128]{2,1,0:T(8,128)S(1)} collective-permute-done((f32[8,72,128]{2,1,0:T(8,128)S(1)}, f32[8,72,128]{2,1,0:T(8,128)S(1)}, u32[]{:S(2)}, u32[]{:S(2)}) %collective-permute-start.3) | collective-permute-done | bytes 294944 | tf_op jit(solution)/shard_map/ppermute | solution.py:406
  36.7 0.0 copy-done.4
  36.7 0.0 copy-start.3
  36.7 1.4 %copy-done.3 = f32[9,8,40,128]{3,2,1,0:T(8,128)S(1)} copy-done((f32[9,8,40,128]{3,2,1,0:T(8,128)S(1)}, f32[9,8,40,128]{3,2,1,0:T(8,128)}, u32[]{:S(2)}) %copy-start.3) | copy-done | bytes 1474584
  38.0 12.6 %shard_map.70 = (f32[256,512]{1,0:T(8,128)}, f32[256,512]{1,0:T(8,128)}) custom-call(f32[8,8,40,128]{3,2,1,0:T(8,128)S(1)} %get-tuple-element.16.s0_in, f32[9,8,40,128]{3,2,1,0:T(8,128)S(1)} %copy-done.3, f32[10,8,40,128]{3,2,1,0:T(8,128)} %get-tuple-element.18.it0_in, f32[4,4,40,128]{3,2,1,0:T(8,128)S(1)} %get-tuple-element.19.s1_in, ...), custom_call_target="tpu_custom_call" | custom-call | tf_op jit(solution)/shard_map/pallas_call | solution.py:477
Async XLA Ops:
  0.6 17.4 %copy-start.2 = (s32[256,512]{1,0:T(8,128)S(1)}, s32[256,512]{1,0:T(8,128)}, u32[]{:S(2)}) copy-start(s32[256,512]{1,0:T(8,128)} %mask.1) | copy-start | bytes 1572868
  0.6 17.4 %copy-start.1 = (s32[256,512]{1,0:T(8,128)S(1)}, s32[256,512]{1,0:T(8,128)}, u32[]{:S(2)}) copy-start(s32[256,512]{1,0:T(8,128)} %depth.1) | copy-start | bytes 1572868
  0.6 17.4 %copy-start = (f32[256,512]{1,0:T(8,128)S(1)}, f32[256,512]{1,0:T(8,128)}, u32[]{:S(2)}) copy-start(f32[256,512]{1,0:T(8,128)} %f.1) | copy-start | bytes 1572868
  2.8 9.3 %collective-permute-start = (f32[2,256,128]{2,1,0:T(8,128)}, f32[2,256,128]{2,1,0:T(8,128)S(1)}, u32[]{:S(2)}, u32[]{:S(2)}) collective-permute-start(f32[2,256,128]{2,1,0:T(8,128)} %get-tuple-element.14), channel_id=1, source_target_pairs={{0,8},{8,0},{16,24},{24,16},{32,40},{40,32},{48,56},{56,48},{64,72... | collective-permute-start | bytes 786440 | tf_op jit(solution)/shard_map/ppermute | solution.py:406
  4.9 31.7 %copy-start.4 = (bf16[1024,512]{1,0:T(8,128)(2,1)S(1)}, bf16[1024,512]{1,0:T(8,128)(2,1)}, u32[]{:S(2)}) copy-start(bf16[1024,512]{1,0:T(8,128)(2,1)} %constant.5.clone.join) | copy-start | bytes 3145732
  4.9 13.1 %collective-permute-start.1 = (f32[2,256,128]{2,1,0:T(8,128)}, f32[2,256,128]{2,1,0:T(8,128)S(1)}, u32[]{:S(2)}, u32[]{:S(2)}) collective-permute-start(f32[2,256,128]{2,1,0:T(8,128)} %get-tuple-element.15), channel_id=1, source_target_pairs={{8,16},{16,8},{24,32},{32,24},{40,48},{48,40},{56,64},{64,56},{72,... | collective-permute-start | bytes 786440 | tf_op jit(solution)/shard_map/ppermute | solution.py:406
  27.1 4.5 %collective-permute-start.2 = (f32[8,72,128]{2,1,0:T(8,128)S(1)}, f32[8,72,128]{2,1,0:T(8,128)S(1)}, u32[]{:S(2)}, u32[]{:S(2)}) collective-permute-start(f32[8,72,128]{2,1,0:T(8,128)S(1)} %get-tuple-element.24), channel_id=1, source_target_pairs={{0,1},{1,0},{2,3},{3,2},{4,5},{5,4},{6,7},{7,6},{8,9},{9,8},{10,11... | collective-permute-start | bytes 884744 | tf_op jit(solution)/shard_map/ppermute | solution.py:406
  28.6 8.0 %collective-permute-start.3 = (f32[8,72,128]{2,1,0:T(8,128)S(1)}, f32[8,72,128]{2,1,0:T(8,128)S(1)}, u32[]{:S(2)}, u32[]{:S(2)}) collective-permute-start(f32[8,72,128]{2,1,0:T(8,128)S(1)} %get-tuple-element.25), channel_id=1, source_target_pairs={{1,2},{2,1},{3,4},{4,3},{5,6},{6,5},{9,10},{10,9},{11,12},{12,11},... | collective-permute-start | bytes 884744 | tf_op jit(solution)/shard_map/ppermute | solution.py:406
  36.7 1.4 %copy-start.3 = (f32[9,8,40,128]{3,2,1,0:T(8,128)S(1)}, f32[9,8,40,128]{3,2,1,0:T(8,128)}, u32[]{:S(2)}) copy-start(f32[9,8,40,128]{3,2,1,0:T(8,128)} %get-tuple-element.17.h0_in) | copy-start | bytes 4423684
where the time goes:
time: 50.9 us; the launch traced here: 50.7 us
  Pallas kernels  23.8 us (47%)
  starting transfers between devices  13.9 us (27%)
  waiting for transfers between devices  10.9 us (21%)
  local copies, waits for them, and re-layouts  1.39 us (3%)
  between operations  0.68 us (1%)
    ppermute x4, starting transfers between devices, swap(): return lax.ppermute(x, axis, pairs)  13.9 us
    pallas_call x1, Pallas kernels, local(): pl.pallas_call(up_kernel, out_shape=[shaped(rows, columns)] * 2, in_specs...  12.6 us
    ppermute x4, waiting for transfers between devices, swap(): return lax.ppermute(x, axis, pairs)  10.9 us
    pallas_call x1, Pallas kernels, local(): pl.pallas_call(down_kernel, out_shape=[shaped(*planes(8)), shaped(*planes...  9.01 us
    pallas_call x1, Pallas kernels, local(): pl.pallas_call(pack_kernel, grid=(1,), out_shape=[shaped(2, rows, SIDE)]...  2.16 us
    unnamed x10, local copies, waits for them, and re-layouts  1.39 us
  transfers between devices with their start and end apart: 4, of which 2 were waited for; matrix products, arithmetic and copies ran while one was open for 0% of the time, Pallas kernels for 0%

commit v1 on v0

--- a/solution.py
+++ b/solution.py
@@ -41,11 +41,8 @@
 
 
 def each(count, body):
-    if count <= 2:
-        for q in range(count):
-            body(q)
-    else:
-        lax.fori_loop(0, count, lambda q, carry: (body(q), carry)[1], 0)
+    for q in range(count):
+        body(q)
 
 
 def whole(ref, q, r):
@@ -371,12 +368,12 @@
         sweep(n, ke, kn, w, k, a, b)
         if n < CELL:
             sweep(n, ke, kn, w, k, b, a)
-        above = lambda q, r, a=a: a[lax.div(q, 2) + 1, r // 2]
+        above = lambda q, r, a=a: a[q // 2 + 1, r // 2]
 
     n, _, ke, kn, _, d, w, k, _, _, a, b, _ = levels[0]
 
     def flatten(q, r, x):
-        flat[pl.ds(pl.multiple_of(q * TALL, 8), TALL), r * LANES : (r + 1) * LANES] = x
+        flat[q * TALL : (q + 1) * TALL, r * LANES : (r + 1) * LANES] = x
 
     def finish(out):
         res = dot_parts(flat[...], join[...])
@@ -435,7 +432,8 @@
     return [pltpu.VMEM(s, jnp.float32) for s in shapes]
 
 
-LIMIT = pltpu.CompilerParams(vmem_limit_bytes=48 * 1024 * 1024)
+def limit(mib):
+    return pltpu.CompilerParams(vmem_limit_bytes=mib * 1024 * 1024)
 
 
 def local(right_side, depth_level, ocean_mask):
@@ -449,9 +447,10 @@
         out_shape=[shaped(2, rows, SIDE)] * 2,
         in_specs=[left, right] * 3,
         out_specs=[VMEM] * 2,
+        compiler_params=limit(8),
     )(right_side, right_side, depth_level, depth_level, ocean_mask, ocean_mask)
+    second = swap(second, "lon", lon, 1, True)
     first = swap(first, "lon", lon, 0, True)
-    second = swap(second, "lon", lon, 1, True)
 
     wide = CELL * LANES
     message = shaped(CELL, 2 * STRIP + 8, LANES)
@@ -469,11 +468,11 @@
             (CELL, TALL * CELL, LANES), (CELL, TALL * CELL, LANES), planes(4, 1), planes(2, 1),
             *[s for n in (8, 4, 2) for s in (planes(n), planes(n, 1), planes(n), planes(n), planes(n), planes(n, 2))],
         ),
-        compiler_params=LIMIT,
+        compiler_params=limit(30),
     )(right_side, depth_level, ocean_mask, first, second, split_matrix(columns))
     *fields, first, second = outs
+    second = swap(second, "lat", lat, 1, False)
     first = swap(first, "lat", lat, 0, False)
-    second = swap(second, "lat", lat, 1, False)
     return pl.pallas_call(
         up_kernel,
         out_shape=[shaped(rows, columns)] * 2,
@@ -492,7 +491,7 @@
             ],
             (TALL * CELL, wide), (columns // LANES, TALL * CELL, LANES),
         ),
-        compiler_params=LIMIT,
+        compiler_params=limit(30),
     )(*fields, first, second, join_matrix(columns))
 
 

time: 50.9 us -> 40.2 us (0.79)
  Pallas kernels: 23.8 us -> 11.4 us
  local copies, waits for them, and re-layouts: 1.39 us -> 3.14 us
    pallas_call x1, Pallas kernels: 12.6 us -> 7 us  [local(): pl.pallas_call(up_kernel, out_shape=[shaped(rows, columns)] * 2, in_specs...]
    pallas_call x1, Pallas kernels: 9.01 us -> 4.33 us  [local(): pl.pallas_call(down_kernel, out_shape=[shaped(*planes(8)), shaped(*planes...]
    pallas_call x1, Pallas kernels: 2.16 us -> 0.1 us  [local(): pl.pallas_call(pack_kernel, grid=(1,), out_shape=[shaped(2, rows, SIDE)]...]
    unnamed x10 -> x16, local copies, waits for them, and re-layouts: 1.39 us -> 3.14 us
where the time goes in v1:
time: 40.2 us; the launch traced here: 40 us
  starting transfers between devices  14 us (35%)
  Pallas kernels  11.4 us (28%)
  waiting for transfers between devices  10.7 us (27%)
  local copies, waits for them, and re-layouts  3.14 us (8%)
  between operations  0.69 us (2%)
    ppermute x4, starting transfers between devices, swap(): return lax.ppermute(x, axis, pairs)  14 us
    ppermute x4, waiting for transfers between devices, swap(): return lax.ppermute(x, axis, pairs)  10.7 us
    pallas_call x1, Pallas kernels, local(): pl.pallas_call(up_kernel, out_shape=[shaped(rows, columns)] * 2, in_specs...  7 us
    pallas_call x1, Pallas kernels, local(): pl.pallas_call(down_kernel, out_shape=[shaped(*planes(8)), shaped(*planes...  4.33 us
    unnamed x16, local copies, waits for them, and re-layouts  3.14 us
  transfers between devices with their start and end apart: 4, of which 2 were waited for; matrix products, arithmetic and copies ran while one was open for 0% of the time, Pallas kernels for 0%

profile of v1, /device:TPU:1, one launch (start us, length us, event | category | flops | bytes accessed | tf_op | source)
XLA Modules:
  0.0 40.0 jit_solution(7727289917910290508)
XLA Ops:
  0.6 0.0 copy-start
  0.6 1.0 %copy-done = f32[256,512]{1,0:T(8,128)S(1)} copy-done((f32[256,512]{1,0:T(8,128)S(1)}, f32[256,512]{1,0:T(8,128)}, u32[]{:S(2)}) %copy-start) | copy-done | bytes 524312
  1.7 0.0 copy-start.2
  1.7 1.0 %copy-done.2 = s32[256,512]{1,0:T(8,128)S(1)} copy-done((s32[256,512]{1,0:T(8,128)S(1)}, s32[256,512]{1,0:T(8,128)}, u32[]{:S(2)}) %copy-start.2) | copy-done | bytes 524312
  2.7 0.0 copy-start.4
  2.7 1.0 %copy-done.4 = s32[256,512]{1,0:T(8,128)S(1)} copy-done((s32[256,512]{1,0:T(8,128)S(1)}, s32[256,512]{1,0:T(8,128)}, u32[]{:S(2)}) %copy-start.4) | copy-done | bytes 524312
  3.8 0.0 copy-start.1
  3.8 0.0 copy-start.3
  3.8 0.0 copy-start.5
  3.8 0.0 copy-start.6
  3.8 0.1 shard_map.68
  3.9 2.2 %collective-permute-start = (f32[2,256,128]{2,1,0:T(8,128)S(1)}, f32[2,256,128]{2,1,0:T(8,128)S(1)}, u32[]{:S(2)}, u32[]{:S(2)}) collective-permute-start(f32[2,256,128]{2,1,0:T(8,128)S(1)} %get-tuple-element.14), channel_id=1, source_target_pairs={{0,8},{8,0},{16,24},{24,16},{32,40},{40,32},{48,56},{56,48},{64,72... | collective-permute-start | bytes 786440 | tf_op jit(solution)/shard_map/ppermute | solution.py:403
  6.1 0.0 copy-start.7
  6.1 7.2 %collective-permute-start.1 = (f32[2,256,128]{2,1,0:T(8,128)S(1)}, f32[2,256,128]{2,1,0:T(8,128)S(1)}, u32[]{:S(2)}, u32[]{:S(2)}) collective-permute-start(f32[2,256,128]{2,1,0:T(8,128)S(1)} %get-tuple-element.15), channel_id=1, source_target_pairs={{8,16},{16,8},{24,32},{32,24},{40,48},{48,40},{56,64},{64,56},{72,... | collective-permute-start | bytes 786440 | tf_op jit(solution)/shard_map/ppermute | solution.py:403
  13.3 0.0 collective-permute-done.first
  13.3 5.7 %collective-permute-done.1.second = f32[2,256,128]{2,1,0:T(8,128)S(1)} collective-permute-done((f32[2,256,128]{2,1,0:T(8,128)S(1)}, f32[2,256,128]{2,1,0:T(8,128)S(1)}, u32[]{:S(2)}, u32[]{:S(2)}) %collective-permute-start.1) | collective-permute-done | bytes 262176 | tf_op jit(solution)/shard_map/ppermute | solution.py:403
  19.0 0.0 copy-done.1
  19.0 0.0 copy-done.3
  19.0 0.0 copy-done.5
  19.0 0.0 copy-done.6
  19.0 4.3 %shard_map.69 = (f32[8,8,40,128]{3,2,1,0:T(8,128)S(1)}, f32[9,8,40,128]{3,2,1,0:T(8,128)S(1)}, f32[10,8,40,128]{3,2,1,0:T(8,128)S(1)}, f32[4,4,40,128]{3,2,1,0:T...) custom-call(f32[256,512]{1,0:T(8,128)S(1)} %copy-done.1, ...), custom_call_target="tpu_custom_call" | custom-call | tf_op jit(solution)/shard_map/pallas_call | solution.py:457
  23.4 1.6 %collective-permute-start.2 = (f32[8,72,128]{2,1,0:T(8,128)S(1)}, f32[8,72,128]{2,1,0:T(8,128)S(1)}, u32[]{:S(2)}, u32[]{:S(2)}) collective-permute-start(f32[8,72,128]{2,1,0:T(8,128)S(1)} %get-tuple-element.24), channel_id=1, source_target_pairs={{0,1},{1,0},{2,3},{3,2},{4,5},{5,4},{6,7},{7,6},{8,9},{9,8},{10,11... | collective-permute-start | bytes 884744 | tf_op jit(solution)/shard_map/ppermute | solution.py:403
  25.0 3.0 %collective-permute-start.3 = (f32[8,72,128]{2,1,0:T(8,128)S(1)}, f32[8,72,128]{2,1,0:T(8,128)S(1)}, u32[]{:S(2)}, u32[]{:S(2)}) collective-permute-start(f32[8,72,128]{2,1,0:T(8,128)S(1)} %get-tuple-element.25), channel_id=1, source_target_pairs={{1,2},{2,1},{3,4},{4,3},{5,6},{6,5},{9,10},{10,9},{11,12},{12,11},... | collective-permute-start | bytes 884744 | tf_op jit(solution)/shard_map/ppermute | solution.py:403
  28.0 0.0 collective-permute-done.2.first
  28.0 5.0 %collective-permute-done.3.second = f32[8,72,128]{2,1,0:T(8,128)S(1)} collective-permute-done((f32[8,72,128]{2,1,0:T(8,128)S(1)}, f32[8,72,128]{2,1,0:T(8,128)S(1)}, u32[]{:S(2)}, u32[]{:S(2)}) %collective-permute-start.3) | collective-permute-done | bytes 294944 | tf_op jit(solution)/shard_map/ppermute | solution.py:403
  33.0 0.0 copy-done.7
  33.0 7.0 %shard_map.70 = (f32[256,512]{1,0:T(8,128)}, f32[256,512]{1,0:T(8,128)}) custom-call(f32[8,8,40,128]{3,2,1,0:T(8,128)S(1)} %get-tuple-element.16.s0_in, f32[9,8,40,128]{3,2,1,0:T(8,128)S(1)} %get-tuple-element.17.h0_in, f32[10,8,40,128]{3,2,1,0:T(8,128)S(1)} %get-tuple-element.18.it0_in, f32[4,4,40,128]{3,2,1,0:T(8,128)S(1)} %get-tuple-element.19.s1_in, ...), custom_call_target="tpu_custom_call" | custom-call | tf_op jit(solution)/shard_map/pallas_call | solution.py:476
Async XLA Ops:
  0.6 1.0 %copy-start = (f32[256,512]{1,0:T(8,128)S(1)}, f32[256,512]{1,0:T(8,128)}, u32[]{:S(2)}) copy-start(f32[256,512]{1,0:T(8,128)} %f.1) | copy-start | bytes 1572868
  1.7 1.0 %copy-start.2 = (s32[256,512]{1,0:T(8,128)S(1)}, s32[256,512]{1,0:T(8,128)}, u32[]{:S(2)}) copy-start(s32[256,512]{1,0:T(8,128)} %depth.1) | copy-start | bytes 1572868
  2.7 1.0 %copy-start.4 = (s32[256,512]{1,0:T(8,128)S(1)}, s32[256,512]{1,0:T(8,128)}, u32[]{:S(2)}) copy-start(s32[256,512]{1,0:T(8,128)} %mask.1) | copy-start | bytes 1572868
  3.8 15.2 %copy-start.1 = (f32[256,512]{1,0:T(8,128)S(1)}, f32[256,512]{1,0:T(8,128)}, u32[]{:S(2)}) copy-start(f32[256,512]{1,0:T(8,128)} %f.1) | copy-start | bytes 1572868
  3.8 15.2 %copy-start.3 = (s32[256,512]{1,0:T(8,128)S(1)}, s32[256,512]{1,0:T(8,128)}, u32[]{:S(2)}) copy-start(s32[256,512]{1,0:T(8,128)} %depth.1) | copy-start | bytes 1572868
  3.8 15.2 %copy-start.5 = (s32[256,512]{1,0:T(8,128)S(1)}, s32[256,512]{1,0:T(8,128)}, u32[]{:S(2)}) copy-start(s32[256,512]{1,0:T(8,128)} %mask.1) | copy-start | bytes 1572868
  3.8 15.2 %copy-start.6 = (bf16[768,1024]{1,0:T(8,128)(2,1)S(1)}, bf16[768,1024]{1,0:T(8,128)(2,1)}, u32[]{:S(2)}) copy-start(bf16[768,1024]{1,0:T(8,128)(2,1)} %constant.4.clone.split) | copy-start | bytes 4718596
  3.9 9.4 %collective-permute-start = (f32[2,256,128]{2,1,0:T(8,128)S(1)}, f32[2,256,128]{2,1,0:T(8,128)S(1)}, u32[]{:S(2)}, u32[]{:S(2)}) collective-permute-start(f32[2,256,128]{2,1,0:T(8,128)S(1)} %get-tuple-element.14), channel_id=1, source_target_pairs={{0,8},{8,0},{16,24},{24,16},{32,40},{40,32},{48,56},{56,48},{64,72... | collective-permute-start | bytes 786440 | tf_op jit(solution)/shard_map/ppermute | solution.py:403
  6.1 26.9 %copy-start.7 = (bf16[1024,512]{1,0:T(8,128)(2,1)S(1)}, bf16[1024,512]{1,0:T(8,128)(2,1)}, u32[]{:S(2)}) copy-start(bf16[1024,512]{1,0:T(8,128)(2,1)} %constant.5.clone.join) | copy-start | bytes 3145732
  6.1 12.9 %collective-permute-start.1 = (f32[2,256,128]{2,1,0:T(8,128)S(1)}, f32[2,256,128]{2,1,0:T(8,128)S(1)}, u32[]{:S(2)}, u32[]{:S(2)}) collective-permute-start(f32[2,256,128]{2,1,0:T(8,128)S(1)} %get-tuple-element.15), channel_id=1, source_target_pairs={{8,16},{16,8},{24,32},{32,24},{40,48},{48,40},{56,64},{64,56},{72,... | collective-permute-start | bytes 786440 | tf_op jit(solution)/shard_map/ppermute | solution.py:403
  23.4 4.6 %collective-permute-start.2 = (f32[8,72,128]{2,1,0:T(8,128)S(1)}, f32[8,72,128]{2,1,0:T(8,128)S(1)}, u32[]{:S(2)}, u32[]{:S(2)}) collective-permute-start(f32[8,72,128]{2,1,0:T(8,128)S(1)} %get-tuple-element.24), channel_id=1, source_target_pairs={{0,1},{1,0},{2,3},{3,2},{4,5},{5,4},{6,7},{7,6},{8,9},{9,8},{10,11... | collective-permute-start | bytes 884744 | tf_op jit(solution)/shard_map/ppermute | solution.py:403
  25.0 8.0 %collective-permute-start.3 = (f32[8,72,128]{2,1,0:T(8,128)S(1)}, f32[8,72,128]{2,1,0:T(8,128)S(1)}, u32[]{:S(2)}, u32[]{:S(2)}) collective-permute-start(f32[8,72,128]{2,1,0:T(8,128)S(1)} %get-tuple-element.25), channel_id=1, source_target_pairs={{1,2},{2,1},{3,4},{4,3},{5,6},{6,5},{9,10},{10,9},{11,12},{12,11},... | collective-permute-start | bytes 884744 | tf_op jit(solution)/shard_map/ppermute | solution.py:403
